TPU v7x, 32 devices: a whole 2x2x4 slice. The times are simulated.
32 devices in a mesh: dp: 8 (over z, core), pos: 4 (over y, x).
Axes of the slice: x: 2, y: 2, z: 4, core: 2. Of those that a mesh axis runs over, the one named last changes fastest.
Arguments:
- features: bfloat16 [64, 128, 224], P(('dp', 'pos')), may hold values from -6 to 6
- counts: int32 [32], P(('dp', 'pos')), may hold values from 1 to 2, as said below
- channel_order: int32 [224], replicated, may hold values from 0 to 223, each once
Outputs:
- mean: float32 [128, 100], P('pos')
- covariance: float32 [128, 100, 100], P('pos')
Inputs may be any that keep to these rules, and one draw needn't show every extreme that they name: `counts`: some device has all 2 slots live and some device only one.
All inputs are finite; a program needn't handle non-finite values.
Results may differ from a plain program's by a relative error of at most 0.0003.
Values may be sent and summed in bfloat16 or wider, within the bound.
No kernel may reach another device: no remote copies, remote signals or barrier semaphores. Data moves between devices by JAX's collectives and lax.ppermute only.
A program may use at most 128 MiB of HBM per device.

v0:
```python
import jax
import jax.numpy as jnp
from jax import lax
from jax.sharding import PartitionSpec as P

CH = 100


def local_stats(received, source_counts, slots, rows, width):
    sources = source_counts.shape[0]
    samples = received.reshape(sources * slots, rows, width).astype(jnp.float32)
    live_mask = (jnp.arange(slots, dtype=jnp.float32)[None, :] < source_counts[:, None]).astype(
        jnp.float32
    )
    live_mask = live_mask.reshape(sources * slots)
    group_count = jnp.sum(source_counts).reshape(1)
    group_sums = jnp.sum(samples, axis=0)
    group_mean = group_sums / group_count
    centered = (samples - group_mean[None]) * live_mask[:, None, None]
    products = jnp.einsum("gpc,gpd->pcd", centered, centered, precision=lax.Precision.HIGHEST)
    return (group_count, group_sums, group_mean, products)


def common_mean(group_count, group_sums, group_mean):
    total_count, total_sums = lax.psum((group_count, group_sums), "dp")
    mean = total_sums / total_count
    offset = group_mean - mean
    weighted = offset * group_count
    return (total_count, mean, offset, weighted)


def on_device(features, counts, channel_order):
    slots, positions, channels = features.shape
    groups = lax.axis_size("pos")
    pos_dev = positions // groups
    kept = channel_order[:CH]
    picker = (kept[None, :] == jnp.arange(channels, dtype=jnp.int32)[:, None]).astype(jnp.bfloat16)
    owned = counts[0]
    slot_live = (jnp.arange(slots, dtype=jnp.int32) < owned).astype(jnp.bfloat16)
    embed = jnp.dot(
        features.reshape(slots * positions, channels), picker, preferred_element_type=jnp.float32
    )
    embed = embed.astype(jnp.bfloat16).reshape(slots, positions, CH) * slot_live[:, None, None]
    identity = jnp.eye(CH, dtype=jnp.float32)
    packed = embed.reshape(slots, groups, pos_dev * CH)
    owned_wire = jnp.broadcast_to(owned.astype(jnp.bfloat16).reshape(1, 1, 1), (1, groups, 1))
    received, source_counts = (
        lax.all_to_all(packed, "pos", split_axis=1, concat_axis=0, tiled=True),
        lax.all_to_all(owned_wire, "pos", split_axis=1, concat_axis=0, tiled=True),
    )
    source_counts = source_counts.reshape(groups).astype(jnp.float32)
    group_count, group_sums, group_mean, products = local_stats(
        received, source_counts, slots, pos_dev, CH
    )
    total_count, mean, offset, weighted = common_mean(group_count, group_sums, group_mean)
    own_term = products + offset[:, :, None] * weighted[:, None, :]
    summed = lax.psum(own_term, "dp")
    covariance = summed / (total_count[0] - 1.0) + 0.01 * identity
    return (mean, covariance)


def solution(mesh):
    in_specs = (P(("dp", "pos"), None, None), P(("dp", "pos")), P())
    out_specs = (P("pos", None), P("pos", None, None))
    return jax.shard_map(
        on_device, mesh=mesh, in_specs=in_specs, out_specs=out_specs, check_vma=False
    )
```

profile of v0, /device:TPU:0, one launch (start us, length us, event | category | flops | bytes accessed | tf_op | source)
XLA Modules:
  0.0 129.7 jit_solution(13337276662901932767)
XLA Ops:
  7.9 0.6 broadcast_in_dim.2
  8.4 5.2 %all-to-all-start.1 = ((bf16[1,4,1]{2,0,1:T(2,128)(2,1)}), bf16[1,4,1]{2,0,1:T(2,128)(2,1)S(1)}, u32[]{:S(2)}, u32[]{:S(2)}) async-start(bf16[1,4,1]{2,0,1:T(2,128)(2,1)} %broadcast_in_dim.2), calls=%async_computation.1 | async-start | bytes 4096 | tf_op jit(solution)/shard_map/all_to_all | solution.py:49
  13.6 0.7 slice.3
  14.3 0.2 fusion
  14.5 0.1 copy.19
  14.6 0.2 reshape.81
  14.8 0.1 broadcast_multiply_fusion
  14.9 0.7 copy.20
  15.6 2.6 %all-to-all-done.1 = bf16[1,4,1]{2,0,1:T(2,128)(2,1)S(1)} async-done(((bf16[1,4,1]{2,0,1:T(2,128)(2,1)}), bf16[1,4,1]{2,0,1:T(2,128)(2,1)S(1)}, u32[]{:S(2)}, u32[]{:S(2)}) %all-to-all-start.1) | async-done | bytes 40 | tf_op jit(solution)/shard_map/all_to_all | solution.py:49
  18.2 3.3 %all-to-all-start = ((bf16[2,4,3200]{2,0,1:T(2,128)(2,1)}), bf16[2,4,3200]{2,0,1:T(2,128)(2,1)S(1)}, u32[]{:S(2)}, u32[]{:S(2)}) async-start(bf16[2,4,3200]{2,0,1:T(2,128)(2,1)} %copy.20), calls=%async_computation | async-start | bytes 102400 | tf_op jit(solution)/shard_map/all_to_all | solution.py:48
  21.5 0.7 convert_reduce_fusion.1
  22.2 0.1 fusion.6
  22.3 0.1 reshape.85
  22.4 3.9 %all-to-all-done = bf16[2,4,3200]{2,0,1:T(2,128)(2,1)S(1)} async-done(((bf16[2,4,3200]{2,0,1:T(2,128)(2,1)}), bf16[2,4,3200]{2,0,1:T(2,128)(2,1)S(1)}, u32[]{:S(2)}, u32[]{:S(2)}) %all-to-all-start) | async-done | bytes 51232 | tf_op jit(solution)/shard_map/all_to_all | solution.py:48
  26.2 0.1 convert_reduce_fusion
  26.3 0.1 reduce_sum.21
  26.5 0.3 reshape.84
  26.7 27.4 %all-reduce = (f32[32,100]{1,0:T(8,128)S(1)}, f32[]{:T(128)}) all-reduce(f32[32,100]{1,0:T(8,128)S(1)} %reduce_sum.21, f32[]{:T(128)} %get-tuple-element.11), channel_id=1, replica_groups=mesh['dp'=8,'pos'=4] {'dp'}, use_global_device_ids=true, to_apply=%region_1.0 | all-reduce | flops 3201 | bytes 25608 | tf_op jit(solution)/shard_map/psum | solution.py:25
  54.2 1.9 %broadcast_multiply_fusion.1 = (f32[32,100]{1,0:T(8,128)S(1)}, f32[32,100]{1,0:T(8,128)S(1)}, f32[32,100]{1,0:T(8,128)S(1)}, f32[32,100]{1,0:T(8,128)}) fusion(f32[]{:T(128)} %get-tuple-element.11, f32[32,100]{1,0:T(8,128)S(1)} %reduce_sum.21, f32[32,100]{1,0:T(8,128)S(1)} %get-tuple-element.12, f32[]{:T(128)} %get-tuple-element.13), kind=kLoop, calls=%fused_computation.15 | loop fusion | flops 12800 | bytes 76808 | tf_op jit(solution)/shard_map/mul | solution.py:28
  56.1 0.1 subtract_multiply_fusion
  56.2 4.4 %multiply_add_fusion = f32[32,100,100]{2,1,0:T(8,128)} fusion(f32[32,100]{1,0:T(8,128)S(1)} %get-tuple-element.14, f32[32,100]{1,0:T(8,128)S(1)} %get-tuple-element.15, f32[8,32,100]{2,1,0:T(8,128)S(1)} %subtract_multiply_fusion), kind=kOutput, calls=%fused_computation.1 | convolution fusion | flops 31360000 | bytes 1408000 | tf_op jit(solution)/shard_map/gpc,gpd->pcd/dot_general | solution.py:20
  61.3 58.5 %all-reduce.3.cloned.1.call-done = f32[32,100,100]{2,1,0:T(8,128)} async-done(((f32[32,100,100]{2,1,0:T(8,128)}), f32[32,100,100]{2,1,0:T(8,128)}) %all-reduce.3.cloned.1.call-update) | async-done | bytes 1280016 | tf_op jit(solution)/shard_map/psum | solution.py:57
  119.8 1.6 %divide_add_fusion = f32[32,100,100]{2,1,0:T(8,128)S(1)} fusion(f32[32,100,100]{2,1,0:T(8,128)} %all-reduce.3.cloned.1.call-done, f32[100,100]{1,0:T(8,128)S(1)} %fusion.5, f32[]{:T(128)S(6)} %sub.17), kind=kLoop, calls=%fused_computation | loop fusion | flops 640000 | bytes 2600004 | tf_op jit(solution)/shard_map/add | solution.py:58
  121.4 1.5 %copy.23 = f32[32,100,100]{2,0,1:T(8,128)} copy(f32[32,100,100]{2,1,0:T(8,128)S(1)} %divide_add_fusion) | data formatting | bytes 2560000
  (7 shorter events, 0.1 us)
Async XLA Ops:
  7.2 7.1 %copy-start = (bf16[2,128,224]{1,2,0:T(8,128)(2,1)S(1)}, bf16[2,128,224]{1,2,0:T(8,128)(2,1)}, u32[]{:S(2)}) copy-start(bf16[2,128,224]{1,2,0:T(8,128)(2,1)} %param.3) | copy-start | bytes 344068
  8.4 9.7 %all-to-all-start.1 = ((bf16[1,4,1]{2,0,1:T(2,128)(2,1)}), bf16[1,4,1]{2,0,1:T(2,128)(2,1)S(1)}, u32[]{:S(2)}, u32[]{:S(2)}) async-start(bf16[1,4,1]{2,0,1:T(2,128)(2,1)} %broadcast_in_dim.2), calls=%async_computation.1 | async-start | bytes 4096 | tf_op jit(solution)/shard_map/all_to_all | solution.py:49
  18.2 8.1 %all-to-all-start = ((bf16[2,4,3200]{2,0,1:T(2,128)(2,1)}), bf16[2,4,3200]{2,0,1:T(2,128)(2,1)S(1)}, u32[]{:S(2)}, u32[]{:S(2)}) async-start(bf16[2,4,3200]{2,0,1:T(2,128)(2,1)} %copy.20), calls=%async_computation | async-start | bytes 102400 | tf_op jit(solution)/shard_map/all_to_all | solution.py:48
  21.5 98.3 %all-reduce.3.cloned.1.call-start = ((), (), s32[]{:S(2)}) async-start(), calls=%async_computation.2 | async-start | bytes 3407872 | tf_op jit(solution)/shard_map/psum | solution.py:57
Sparse Core Ops, SparseCore 0:
  60.7 59.0 all-reduce.2
where the time goes:
time: 130 us
  waiting for transfers between devices  65 us (50%)
  blocking collectives  27.4 us (21%)
  between operations  15.4 us (12%)
  starting transfers between devices  8.48 us (7%)
  other arithmetic  4.59 us (4%)
  matrix products  4.57 us (4%)
  local copies, waits for them, and re-layouts  4.13 us (3%)
    psum x1, waiting for transfers between devices, on_device(): summed = lax.psum(own_term, 'dp')  58.5 us
    psum x1, blocking collectives, common_mean(): total_count, total_sums = lax.psum((group_count, group_sums), 'dp')  27.4 us
    all_to_all x1, starting transfers between devices, on_device(): lax.all_to_all(owned_wire, 'pos', split_axis=1, concat_axis=0, tiled=True)  5.16 us
    dot_general x1, matrix products, local_stats(): jnp.einsum('gpc,gpd->pcd', centered, centered, precision=lax.Precision.HI...  4.36 us
    all_to_all x1, waiting for transfers between devices, on_device(): lax.all_to_all(packed, 'pos', split_axis=1, concat_axis=0, tiled=True)  3.88 us
    all_to_all x1, starting transfers between devices, on_device(): lax.all_to_all(packed, 'pos', split_axis=1, concat_axis=0, tiled=True)  3.28 us
    all_to_all x1, waiting for transfers between devices, on_device(): lax.all_to_all(owned_wire, 'pos', split_axis=1, concat_axis=0, tiled=True)  2.61 us
  transfers between devices with their start and end apart: 3, of which 3 were waited for; matrix products, arithmetic and copies ran while one was open for 2% of the time, Pallas kernels for 0%

commit v1 on v0

--- a/solution.py
+++ b/solution.py
@@ -4,6 +4,22 @@
 from jax.sharding import PartitionSpec as P
 
 CH = 100
+
+
+def exchange_in_pairs(value, axis, split, join):
+    ways, here = (lax.axis_size(axis), lax.axis_index(axis))
+    width = value.shape[split] // ways
+    shape = list(value.shape)
+    shape[split] = width
+    height = shape[join]
+    shape[join] = height * ways
+    full = jnp.zeros(shape, value.dtype)
+    for mask in range(ways):
+        part = lax.dynamic_slice_in_dim(value, (here ^ mask) * width, width, axis=split)
+        if mask:
+            part = lax.ppermute(part, axis, [(d, d ^ mask) for d in range(ways)])
+        full = lax.dynamic_update_slice_in_dim(full, part, (here ^ mask) * height, axis=join)
+    return full
 
 
 def local_stats(received, source_counts, slots, rows, width):
@@ -46,7 +62,7 @@
     owned_wire = jnp.broadcast_to(owned.astype(jnp.bfloat16).reshape(1, 1, 1), (1, groups, 1))
     received, source_counts = (
         lax.all_to_all(packed, "pos", split_axis=1, concat_axis=0, tiled=True),
-        lax.all_to_all(owned_wire, "pos", split_axis=1, concat_axis=0, tiled=True),
+        exchange_in_pairs(owned_wire, "pos", 1, 0),
     )
     source_counts = source_counts.reshape(groups).astype(jnp.float32)
     group_count, group_sums, group_mean, products = local_stats(

time: 130 us -> 131 us (level)
  waiting for transfers between devices: 65 us -> 60.7 us
  starting transfers between devices: 8.48 us -> 12.6 us
  local copies, waits for them, and re-layouts: 4.13 us -> 5.84 us
    ppermute x0 -> x3, starting transfers between devices: none -> 8.42 us  [exchange_in_pairs(): part = lax.ppermute(part, axis, [(d, d ^ mask) for d in range(ways)])]
    all_to_all x1 -> x0, starting transfers between devices: 5.16 us -> none  [on_device(): lax.all_to_all(owned_wire, 'pos', split_axis=1, concat_axis=0, tiled=True)]
    all_to_all x1 -> x0, waiting for transfers between devices: 2.61 us -> none  [on_device(): lax.all_to_all(owned_wire, 'pos', split_axis=1, concat_axis=0, tiled=True)]
    dynamic_update_slice x0 -> x4, local copies, waits for them, and re-layouts: none -> 2.29 us  [exchange_in_pairs(): lax.dynamic_update_slice_in_dim(full, part, (here ^ mask) * height, axis=...]
    all_to_all x1, waiting for transfers between devices: 3.88 us -> 1.66 us  [on_device(): lax.all_to_all(packed, 'pos', split_axis=1, concat_axis=0, tiled=True)]
  transfers between devices with their start and end apart: 3 -> 5, of which waited for: 3 -> 2; matrix products, arithmetic and copies ran while one was open for 2% -> 4% of each run, Pallas kernels for 0% -> 0%
where the time goes in v1:
time: 131 us
  waiting for transfers between devices  60.7 us (46%)
  blocking collectives  27.2 us (21%)
  between operations  15.4 us (12%)
  starting transfers between devices  12.6 us (10%)
  local copies, waits for them, and re-layouts  5.84 us (4%)
  other arithmetic  4.6 us (4%)
  matrix products  4.57 us (3%)
    psum x1, waiting for transfers between devices, on_device(): summed = lax.psum(own_term, 'dp')  59 us
    psum x1, blocking collectives, common_mean(): total_count, total_sums = lax.psum((group_count, group_sums), 'dp')  27.2 us
    ppermute x3, starting transfers between devices, exchange_in_pairs(): part = lax.ppermute(part, axis, [(d, d ^ mask) for d in range(ways)])  8.42 us
    dot_general x1, matrix products, local_stats(): jnp.einsum('gpc,gpd->pcd', centered, centered, precision=lax.Precision.HI...  4.36 us
    all_to_all x1, starting transfers between devices, on_device(): lax.all_to_all(packed, 'pos', split_axis=1, concat_axis=0, tiled=True)  4.19 us
  transfers between devices with their start and end apart: 5, of which 2 were waited for; matrix products, arithmetic and copies ran while one was open for 4% of the time, Pallas kernels for 0%

profile of v1, /device:TPU:0, one launch (start us, length us, event | category | flops | bytes accessed | tf_op | source)
XLA Modules:
  0.0 130.9 jit_solution(3209055383485276755)
XLA Ops:
  7.9 4.3 %collective-permute-start = (bf16[1,1,1]{2,1,0:T(2,128)(2,1)}, bf16[1,1,1]{2,1,0:T(2,128)(2,1)}, u32[]{:S(2)}, u32[]{:S(2)}) collective-permute-start(bf16[1,1,1]{2,1,0:T(2,128)(2,1)} %bitcast.3), channel_id=1, source_target_pairs={{0,1},{1,0},{2,3},{3,2},{4,5},{5,4},{6,7},{7,6},{8,9},{9,8},{10,11... | collective-permute-start | bytes 14 | tf_op jit(solution)/shard_map/ppermute | solution.py:20
  12.2 2.8 %collective-permute-start.1 = (bf16[1,1,1]{2,1,0:T(2,128)(2,1)}, bf16[1,1,1]{2,1,0:T(2,128)(2,1)}, u32[]{:S(2)}, u32[]{:S(2)}) collective-permute-start(bf16[1,1,1]{2,1,0:T(2,128)(2,1)} %bitcast.3), channel_id=1, source_target_pairs={{0,2},{1,3},{2,0},{3,1},{4,6},{5,7},{6,4},{7,5},{8,10},{9,11},{10,... | collective-permute-start | bytes 14 | tf_op jit(solution)/shard_map/ppermute | solution.py:20
  15.0 1.3 collective-permute-start.2
  16.3 0.7 slice.3
  17.0 0.2 fusion
  17.2 0.1 copy.13
  17.3 0.2 reshape.94
  17.5 0.1 broadcast_multiply_fusion
  17.6 0.7 copy.14
  18.2 4.2 %all-to-all-start = ((bf16[2,4,3200]{2,0,1:T(2,128)(2,1)}), bf16[2,4,3200]{2,0,1:T(2,128)(2,1)S(1)}, u32[]{:S(2)}, u32[]{:S(2)}) async-start(bf16[2,4,3200]{2,0,1:T(2,128)(2,1)} %copy.14), calls=%async_computation | async-start | bytes 102400 | tf_op jit(solution)/shard_map/all_to_all | solution.py:64
  22.4 0.1 dynamic_update_slice.16
  22.6 0.7 dynamic_update_slice.17
  23.3 0.7 dynamic_update_slice.18
  24.1 0.7 dynamic_update_slice.19
  24.8 0.7 convert_reduce_fusion.1
  25.6 1.7 %all-to-all-done = bf16[2,4,3200]{2,0,1:T(2,128)(2,1)S(1)} async-done(((bf16[2,4,3200]{2,0,1:T(2,128)(2,1)}), bf16[2,4,3200]{2,0,1:T(2,128)(2,1)S(1)}, u32[]{:S(2)}, u32[]{:S(2)}) %all-to-all-start) | async-done | bytes 51232 | tf_op jit(solution)/shard_map/all_to_all | solution.py:64
  27.3 0.1 reduce_sum.21
  27.5 0.3 reshape.102
  27.7 27.2 %all-reduce = (f32[32,100]{1,0:T(8,128)S(1)}, f32[]{:T(128)}) all-reduce(f32[32,100]{1,0:T(8,128)S(1)} %reduce_sum.21, f32[]{:T(128)} %convert_reduce_fusion.1), channel_id=1, replica_groups=mesh['dp'=8,'pos'=4] {'dp'}, use_global_device_ids=true, to_apply=%region_1.0 | all-reduce | flops 3201 | bytes 25608 | tf_op jit(solution)/shard_map/psum | solution.py:41
  54.9 1.9 %broadcast_multiply_fusion.1 = (f32[32,100]{1,0:T(8,128)S(1)}, f32[32,100]{1,0:T(8,128)S(1)}, f32[32,100]{1,0:T(8,128)S(1)}, f32[32,100]{1,0:T(8,128)}) fusion(f32[]{:T(128)} %convert_reduce_fusion.1, f32[32,100]{1,0:T(8,128)S(1)} %reduce_sum.21, f32[32,100]{1,0:T(8,128)S(1)} %get-tuple-element.8, f32[]{:T(128)} %get-tuple-element.9), kind=kLoop, calls=%fused_computation.15 | loop fusion | flops 12800 | bytes 76808 | tf_op jit(solution)/shard_map/mul | solution.py:44
  56.9 4.4 %multiply_add_fusion = f32[32,100,100]{2,1,0:T(8,128)} fusion(f32[32,100]{1,0:T(8,128)S(1)} %get-tuple-element.10, f32[32,100]{1,0:T(8,128)S(1)} %get-tuple-element.11, f32[8,32,100]{2,1,0:T(8,128)S(1)} %subtract_multiply_fusion), kind=kOutput, calls=%fused_computation.1 | convolution fusion | flops 31360000 | bytes 1408000 | tf_op jit(solution)/shard_map/gpc,gpd->pcd/dot_general | solution.py:36
  62.0 59.0 %all-reduce.3.cloned.1.call-done = f32[32,100,100]{2,1,0:T(8,128)} async-done(((f32[32,100,100]{2,1,0:T(8,128)}), f32[32,100,100]{2,1,0:T(8,128)}) %all-reduce.3.cloned.1.call-update) | async-done | bytes 1280016 | tf_op jit(solution)/shard_map/psum | solution.py:73
  121.0 1.6 %divide_add_fusion = f32[32,100,100]{2,1,0:T(8,128)S(1)} fusion(f32[32,100,100]{2,1,0:T(8,128)} %all-reduce.3.cloned.1.call-done, f32[100,100]{1,0:T(8,128)S(1)} %fusion.5, f32[]{:T(128)S(6)} %sub.17), kind=kLoop, calls=%fused_computation | loop fusion | flops 640000 | bytes 2600004 | tf_op jit(solution)/shard_map/add | solution.py:74
  122.6 1.5 %copy.17 = f32[32,100,100]{2,0,1:T(8,128)} copy(f32[32,100,100]{2,1,0:T(8,128)S(1)} %divide_add_fusion) | data formatting | bytes 2560000
  (16 shorter events, 0.4 us)
Async XLA Ops:
  7.2 9.8 %copy-start = (bf16[2,128,224]{1,2,0:T(8,128)(2,1)S(1)}, bf16[2,128,224]{1,2,0:T(8,128)(2,1)}, u32[]{:S(2)}) copy-start(bf16[2,128,224]{1,2,0:T(8,128)(2,1)} %param.3) | copy-start | bytes 344068
  7.9 14.7 %collective-permute-start = (bf16[1,1,1]{2,1,0:T(2,128)(2,1)}, bf16[1,1,1]{2,1,0:T(2,128)(2,1)}, u32[]{:S(2)}, u32[]{:S(2)}) collective-permute-start(bf16[1,1,1]{2,1,0:T(2,128)(2,1)} %bitcast.3), channel_id=1, source_target_pairs={{0,1},{1,0},{2,3},{3,2},{4,5},{5,4},{6,7},{7,6},{8,9},{9,8},{10,11... | collective-permute-start | bytes 14 | tf_op jit(solution)/shard_map/ppermute | solution.py:20
  12.2 11.1 %collective-permute-start.1 = (bf16[1,1,1]{2,1,0:T(2,128)(2,1)}, bf16[1,1,1]{2,1,0:T(2,128)(2,1)}, u32[]{:S(2)}, u32[]{:S(2)}) collective-permute-start(bf16[1,1,1]{2,1,0:T(2,128)(2,1)} %bitcast.3), channel_id=1, source_target_pairs={{0,2},{1,3},{2,0},{3,1},{4,6},{5,7},{6,4},{7,5},{8,10},{9,11},{10,... | collective-permute-start | bytes 14 | tf_op jit(solution)/shard_map/ppermute | solution.py:20
  15.0 9.1 %collective-permute-start.2 = (bf16[1,1,1]{2,1,0:T(2,128)(2,1)}, bf16[1,1,1]{2,1,0:T(2,128)(2,1)}, u32[]{:S(2)}, u32[]{:S(2)}) collective-permute-start(bf16[1,1,1]{2,1,0:T(2,128)(2,1)} %bitcast.3), channel_id=1, source_target_pairs={{0,3},{1,2},{2,1},{3,0},{4,7},{5,6},{6,5},{7,4},{8,11},{9,10},{10,... | collective-permute-start | bytes 14 | tf_op jit(solution)/shard_map/ppermute | solution.py:20
  18.2 9.0 %all-to-all-start = ((bf16[2,4,3200]{2,0,1:T(2,128)(2,1)}), bf16[2,4,3200]{2,0,1:T(2,128)(2,1)S(1)}, u32[]{:S(2)}, u32[]{:S(2)}) async-start(bf16[2,4,3200]{2,0,1:T(2,128)(2,1)} %copy.14), calls=%async_computation | async-start | bytes 102400 | tf_op jit(solution)/shard_map/all_to_all | solution.py:64
  22.4 98.5 %all-reduce.3.cloned.1.call-start = ((), (), s32[]{:S(2)}) async-start(), calls=%async_computation.1 | async-start | bytes 3407872 | tf_op jit(solution)/shard_map/psum | solution.py:73
Sparse Core Ops, SparseCore 0:
  61.5 59.4 all-reduce.2

commit v2 on v0

--- a/solution.py
+++ b/solution.py
@@ -54,7 +54,7 @@
     )
     total_count, mean, offset, weighted = common_mean(group_count, group_sums, group_mean)
     own_term = products + offset[:, :, None] * weighted[:, None, :]
-    summed = lax.psum(own_term, "dp")
+    summed = jnp.sum(lax.all_gather(own_term, "dp"), axis=0)
     covariance = summed / (total_count[0] - 1.0) + 0.01 * identity
     return (mean, covariance)
 

time: 130 us -> 195 us (1.50)
  waiting for transfers between devices: 65 us -> 124 us
  other arithmetic: 4.59 us -> 10.6 us
    all_gather x0 -> x1, waiting for transfers between devices: none -> 117 us  [on_device(): summed = jnp.sum(lax.all_gather(own_term, 'dp'), axis=0)]
    psum x1 -> x0, waiting for transfers between devices: 58.5 us -> none  [on_device(): summed = lax.psum(own_term, 'dp')]
    reduce_sum x0 -> x1, other arithmetic: none -> 6.72 us  [on_device(): summed = jnp.sum(lax.all_gather(own_term, 'dp'), axis=0)]
  transfers between devices with their start and end apart: 3 -> 3, of which waited for: 3 -> 3; matrix products, arithmetic and copies ran while one was open for 2% -> 1% of each run, Pallas kernels for 0% -> 0%
where the time goes in v2:
time: 195 us
  waiting for transfers between devices  124 us (64%)
  blocking collectives  27.5 us (14%)
  between operations  15.4 us (8%)
  other arithmetic  10.6 us (5%)
  starting transfers between devices  8.48 us (4%)
  local copies, waits for them, and re-layouts  5.59 us (3%)
  matrix products  3.42 us (2%)
    all_gather x1, waiting for transfers between devices, on_device(): summed = jnp.sum(lax.all_gather(own_term, 'dp'), axis=0)  117 us
    psum x1, blocking collectives, common_mean(): total_count, total_sums = lax.psum((group_count, group_sums), 'dp')  27.5 us
    reduce_sum x1, other arithmetic, on_device(): summed = jnp.sum(lax.all_gather(own_term, 'dp'), axis=0)  6.72 us
    all_to_all x1, starting transfers between devices, on_device(): lax.all_to_all(owned_wire, 'pos', split_axis=1, concat_axis=0, tiled=True)  5.16 us
  transfers between devices with their start and end apart: 3, of which 3 were waited for; matrix products, arithmetic and copies ran while one was open for 1% of the time, Pallas kernels for 0%

profile of v2, /device:TPU:0, one launch (start us, length us, event | category | flops | bytes accessed | tf_op | source)
XLA Modules:
  0.0 194.6 jit_solution(15533061077341183164)
XLA Ops:
  7.9 0.6 broadcast_in_dim.2
  8.4 5.2 %all-to-all-start.1 = ((bf16[1,4,1]{2,0,1:T(2,128)(2,1)}), bf16[1,4,1]{2,0,1:T(2,128)(2,1)S(1)}, u32[]{:S(2)}, u32[]{:S(2)}) async-start(bf16[1,4,1]{2,0,1:T(2,128)(2,1)} %broadcast_in_dim.2), calls=%async_computation.1 | async-start | bytes 4096 | tf_op jit(solution)/shard_map/all_to_all | solution.py:49
  13.6 0.7 slice.3
  14.3 0.2 fusion.1
  14.5 0.1 copy.19
  14.6 0.2 reshape.81
  14.8 0.1 broadcast_multiply_fusion
  14.9 0.7 copy.20
  15.6 2.6 %all-to-all-done.1 = bf16[1,4,1]{2,0,1:T(2,128)(2,1)S(1)} async-done(((bf16[1,4,1]{2,0,1:T(2,128)(2,1)}), bf16[1,4,1]{2,0,1:T(2,128)(2,1)S(1)}, u32[]{:S(2)}, u32[]{:S(2)}) %all-to-all-start.1) | async-done | bytes 40 | tf_op jit(solution)/shard_map/all_to_all | solution.py:49
  18.2 3.3 %all-to-all-start = ((bf16[2,4,3200]{2,0,1:T(2,128)(2,1)}), bf16[2,4,3200]{2,0,1:T(2,128)(2,1)S(1)}, u32[]{:S(2)}, u32[]{:S(2)}) async-start(bf16[2,4,3200]{2,0,1:T(2,128)(2,1)} %copy.20), calls=%async_computation | async-start | bytes 102400 | tf_op jit(solution)/shard_map/all_to_all | solution.py:48
  21.5 0.7 convert_reduce_fusion.1
  22.3 0.1 reshape.85
  22.4 3.9 %all-to-all-done = bf16[2,4,3200]{2,0,1:T(2,128)(2,1)S(1)} async-done(((bf16[2,4,3200]{2,0,1:T(2,128)(2,1)}), bf16[2,4,3200]{2,0,1:T(2,128)(2,1)S(1)}, u32[]{:S(2)}, u32[]{:S(2)}) %all-to-all-start) | async-done | bytes 51232 | tf_op jit(solution)/shard_map/all_to_all | solution.py:48
  26.3 0.1 reduce_sum.30
  26.5 0.3 reshape.84
  26.7 27.5 %all-reduce = (f32[32,100]{1,0:T(8,128)S(1)}, f32[]{:T(128)}) all-reduce(f32[32,100]{1,0:T(8,128)S(1)} %reduce_sum.30, f32[]{:T(128)} %get-tuple-element.7), channel_id=1, replica_groups=mesh['dp'=8,'pos'=4] {'dp'}, use_global_device_ids=true, to_apply=%region_1.0 | all-reduce | flops 3201 | bytes 25608 | tf_op jit(solution)/shard_map/psum | solution.py:25
  54.2 1.9 broadcast_multiply_fusion.1
  56.1 0.1 subtract_multiply_fusion
  56.2 3.2 %multiply_add_fusion = f32[32,100,100]{2,1,0:T(8,128)S(1)} fusion(f32[32,100]{1,0:T(8,128)S(1)} %get-tuple-element.10, f32[32,100]{1,0:T(8,128)S(1)} %get-tuple-element.11, f32[8,32,100]{2,1,0:T(8,128)S(1)} %subtract_multiply_fusion), kind=kOutput, calls=%fused_computation.2 | convolution fusion | flops 31360000 | bytes 1408000 | tf_op jit(solution)/shard_map/gpc,gpd->pcd/dot_general | solution.py:20
  59.4 1.5 copy.23
  61.5 117.0 %all-gather.3.cloned.1.call-done = f32[256,100,100]{2,0,1:T(8,128)} async-done(((f32[32,100,100]{2,0,1:T(8,128)}), f32[256,100,100]{2,0,1:T(8,128)}) %all-gather.3.cloned.1.call-update) | async-done | bytes 10240016 | tf_op jit(solution)/shard_map/all_gather | solution.py:57
  178.6 6.7 %reduce_sum.32 = f32[32,100,100]{2,0,1:T(8,128)S(1)} reduce(f32[8,32,100,100]{3,1,0,2:T(8,128)} %bitcast.19, f32[]{:T(128)} %constant.2.clone.1), dimensions={0}, to_apply=%region_4.0 | reduce | flops 2240000 | bytes 11520004 | tf_op jit(solution)/shard_map/reduce_sum | solution.py:57
  185.3 1.0 fusion
  186.3 1.5 copy.25
  (9 shorter events, 0.3 us)
Async XLA Ops:
  7.2 7.1 %copy-start = (bf16[2,128,224]{1,2,0:T(8,128)(2,1)S(1)}, bf16[2,128,224]{1,2,0:T(8,128)(2,1)}, u32[]{:S(2)}) copy-start(bf16[2,128,224]{1,2,0:T(8,128)(2,1)} %param.3) | copy-start | bytes 344068
  8.4 9.7 %all-to-all-start.1 = ((bf16[1,4,1]{2,0,1:T(2,128)(2,1)}), bf16[1,4,1]{2,0,1:T(2,128)(2,1)S(1)}, u32[]{:S(2)}, u32[]{:S(2)}) async-start(bf16[1,4,1]{2,0,1:T(2,128)(2,1)} %broadcast_in_dim.2), calls=%async_computation.1 | async-start | bytes 4096 | tf_op jit(solution)/shard_map/all_to_all | solution.py:49
  18.2 8.1 %all-to-all-start = ((bf16[2,4,3200]{2,0,1:T(2,128)(2,1)}), bf16[2,4,3200]{2,0,1:T(2,128)(2,1)S(1)}, u32[]{:S(2)}, u32[]{:S(2)}) async-start(bf16[2,4,3200]{2,0,1:T(2,128)(2,1)} %copy.20), calls=%async_computation | async-start | bytes 102400 | tf_op jit(solution)/shard_map/all_to_all | solution.py:48
  21.5 157.1 %all-gather.3.cloned.1.call-start = ((), (), s32[]{:S(2)}) async-start(), calls=%async_computation.2 | async-start | bytes 14745600 | tf_op jit(solution)/shard_map/all_gather | solution.py:57
Sparse Core Ops, SparseCore 0:
  61.0 117.4 all-gather.2
